TPU v7x, 256 devices: a whole 4x4x8 slice. The times are simulated.
256 devices in a mesh: dp: 8 (over y, z_hi), owner: 32 (over x, z_lo, core).
Axes of the slice: x: 4, y: 4, z: 8 (z_hi: 2, z_lo: 4; z = z_hi * 4 + z_lo), core: 2. Of those that a mesh axis runs over, the one named last changes fastest.
Arguments:
- grad_parts: bfloat16 [8, 128, 512, 512], P('dp', None, 'owner'), may hold values from -2.5 to 2.5
- stats: float32 [256, 512, 512], P(('dp', 'owner')), may hold values from -10 to 12, as said below
- roots: bfloat16 [256, 512, 512], P(('dp', 'owner')), may hold values from -0.25 to 0.25
- refresh: int32 [128], P('dp'), may hold values 0 or 1
Outputs:
- new_stats: float32 [256, 512, 512], P(('dp', 'owner'))
- new_roots: bfloat16 [256, 512, 512], P(('dp', 'owner'))
- update: bfloat16 [128, 512, 512], P('dp', 'owner')
Inputs may be any that keep to these rules, and one draw needn't show every extreme that they name: Every stats matrix is symmetric positive definite.
All inputs are finite; a program needn't handle non-finite values. No bound on the sum of `refresh` on one device may be relied on, other than what follows from the above.
Results may differ from a plain program's by a relative error of at most 0.015.
Values may be sent and summed in bfloat16 or wider, within the bound.
A program may use at most 64 MiB of HBM per device.

v0:
```python
import jax
import jax.numpy as jnp
from jax import lax
from jax.sharding import PartitionSpec as P

ITERS = 5
BETA = 0.8


def split_up(x, dim, peers):
    before, after = (x.shape[:dim], x.shape[dim + 1 :])
    return jnp.moveaxis(x.reshape(*before, peers, -1, *after), dim, 0)


def summed_on_arrival(x, axis, dim):
    pieces = split_up(x, dim, lax.axis_size(axis))
    arrived = lax.all_to_all(pieces, axis, split_axis=0, concat_axis=0, tiled=True)
    return arrived.astype(jnp.float32).sum(axis=0)


def partner_2(value, axis, stride):
    mask = 2**stride
    pairs = [(source, source ^ mask) for source in range(lax.axis_size(axis))]
    return lax.ppermute(value, axis, pairs)


def inverse_root(matrix):
    size = matrix.shape[0]
    eye = jnp.eye(size, dtype=jnp.float32)
    scale = jnp.sqrt(jnp.sum(matrix * matrix) + 1e-06)
    current = matrix / scale
    result = eye * scale ** (-0.25)
    for step in range(ITERS):
        factor = (5.0 * eye - current) / 4.0
        result = jnp.dot(result, factor, precision=lax.Precision.HIGHEST)
        if step + 1 < ITERS:
            square = jnp.dot(factor, factor, precision=lax.Precision.HIGHEST)
            fourth = jnp.dot(square, square, precision=lax.Precision.HIGHEST)
            current = jnp.dot(fourth, current, precision=lax.Precision.HIGHEST)
    return result


def local(grad_parts, stats, roots, refresh):
    summed = summed_on_arrival(grad_parts, "dp", 1)
    grad = summed[0].astype(jnp.bfloat16)
    blocks, rows, width = grad.shape
    owner = lax.axis_index("owner")
    side = owner % 2
    flag = lax.dynamic_index_in_dim(refresh, owner // 2, 0, keepdims=False)
    doubled = jnp.repeat(grad, 2, axis=0)
    whole = lax.all_to_all(doubled, "owner", split_axis=0, concat_axis=1, tiled=True)[0]
    oriented = jnp.where(side == 0, whole, whole.T)
    gram = jnp.dot(oriented, oriented.T, preferred_element_type=jnp.float32)
    partner = partner_2(roots, "owner", 0)[0]
    left_root = jnp.where(side == 0, roots[0], partner)
    right_root = jnp.where(side == 0, partner, roots[0])
    product = jnp.dot(left_root, whole, preferred_element_type=jnp.float32).astype(jnp.bfloat16)
    half = width // 2
    right_half = lax.dynamic_slice_in_dim(right_root, side * half, half, 1)
    portion = jnp.dot(product, right_half, preferred_element_type=jnp.float32).astype(jnp.bfloat16)
    moved = lax.all_to_all(portion[None], "owner", split_axis=1, concat_axis=0, tiled=True)
    update = moved.reshape(blocks, 2, rows, half).transpose(0, 2, 1, 3).reshape(blocks, rows, width)
    fresh = BETA * stats[0] + (1.0 - BETA) * (gram / width)
    solved = inverse_root(fresh)
    chosen = jnp.where(flag == 1, solved.astype(jnp.bfloat16), roots[0])
    return (fresh[None], chosen[None], update)


def solution(mesh):
    placed = (
        P("dp", None, "owner", None),
        P(("dp", "owner"), None, None),
        P(("dp", "owner"), None, None),
        P("dp"),
    )
    return jax.shard_map(
        local,
        mesh=mesh,
        in_specs=placed,
        out_specs=(
            P(("dp", "owner"), None, None),
            P(("dp", "owner"), None, None),
            P("dp", "owner", None),
        ),
        check_vma=False,
    )
```

profile of v0, /device:TPU:1, one launch (start us, length us, event | category | flops | bytes accessed | tf_op | source)
XLA Modules:
  0.0 136.4 jit_solution(5005526059796600987)
XLA Ops:
  0.6 47.6 %all_to_all.23 = bf16[8,1,16,16,512]{4,3,2,1,0:T(8,128)(2,1)S(1)} all-to-all(bf16[8,1,16,16,512]{4,3,2,1,0:T(8,128)(2,1)} %bitcast.57), channel_id=1, replica_groups=mesh['dp'=8,'owner'=32] {'dp'}, dimensions={0} | all-to-all | bytes 4194304 | tf_op jit(solution)/shard_map/all_to_all | solution.py:17
  48.2 0.0 copy-start.3
  48.2 0.0 copy-start
  48.2 0.4 reduce_sum.21
  48.6 0.9 broadcast_in_dim.12
  49.4 23.7 %all-to-all-start.1 = ((bf16[32,16,512]{2,1,0:T(8,128)(2,1)}), bf16[32,16,512]{2,1,0:T(8,128)(2,1)S(1)}, u32[]{:S(2)}, u32[]{:S(2)}) async-start(bf16[32,16,512]{2,1,0:T(8,128)(2,1)} %bitcast.2), calls=%async_computation.1 | async-start | bytes 1048576 | tf_op jit(solution)/shard_map/all_to_all | solution.py:51
  73.1 0.3 collective-permute-start
  73.5 0.0 copy-done.3
  73.5 0.6 dynamic_slice.7
  74.7 15.2 %all-to-all-done.1 = bf16[32,16,512]{2,1,0:T(8,128)(2,1)S(1)} async-done(((bf16[32,16,512]{2,1,0:T(8,128)(2,1)}), bf16[32,16,512]{2,1,0:T(8,128)(2,1)S(1)}, u32[]{:S(2)}, u32[]{:S(2)}) %all-to-all-start.1) | async-done | bytes 524320 | tf_op jit(solution)/shard_map/all_to_all | solution.py:51
  89.9 0.2 copy.16
  90.2 0.0 copy-done
  90.2 1.2 multiply_reduce_fusion
  91.4 0.0 copy-start.1
  92.1 0.0 collective-permute-done
  92.1 1.9 %fusion.6 = bf16[1,512,256]{2,1,0:T(8,128)(2,1)S(1)} fusion(bf16[512,512]{1,0:T(8,128)(2,1)S(1)} %bitcast.55, bf16[1,512,512]{2,1,0:T(8,128)(2,1)} %param.6, bf16[1,512,512]{2,1,0:T(8,128)(2,1)} %collective-permute-done, pred[]{:T(512)S(6)} %eq.26, bf16[512,512]{1,0:T(8,128)(2,1)} %bitcast.61, s32[]{:T(128)S(6)} %select_n.56, bf16[512,512]{1,0:T(8,128)(2,1)} %bitcast.10), kind=kOutput, calls=%fused_computation.14 | convolution fusion | flops 403439616 | bytes 2360832 | tf_op jit(solution)/shard_map/dot_general | solution.py:60
  94.0 0.4 copy.22
  94.5 0.5 broadcast.126
  95.0 2.2 %reduce.2 = bf16[512,256]{1,0:T(8,128)(2,1)S(1)} reduce(bf16[512,1,256]{2,1,0:T(2,128)(2,1)S(1)} %bitcast.58, bf16[]{:T(256)} %broadcast.126), dimensions={1}, to_apply=%bitcast.52.reduce_sub_computation | reduce | bytes 524290
  97.2 0.8 reshape.33
  98.0 3.9 %all-to-all-start.2 = ((bf16[32,2,2048]{2,1,0:T(2,128)(2,1)}), bf16[32,2,2048]{2,1,0:T(2,128)(2,1)S(1)}, u32[]{:S(2)}, u32[]{:S(2)}) async-start(bf16[32,2,2048]{2,1,0:T(2,128)(2,1)} %reshape.33), calls=%async_computation.2 | async-start | bytes 524288 | tf_op jit(solution)/shard_map/all_to_all | solution.py:61
  101.9 2.0 %fusion.25 = f32[512,512]{1,0:T(8,128)S(1)} fusion(f32[512,512]{1,0:T(8,128)S(1)} %get-tuple-element.4, f32[]{:T(128)S(6)} %sqrt.3), kind=kOutput, calls=%fused_computation.29 | convolution fusion | flops 1611923456 | bytes 2097156 | tf_op jit(solution)/shard_map/dot_general | solution.py:37
  103.9 1.9 %fusion.11 = f32[512,512]{1,0:T(8,128)S(1)} fusion(f32[]{:T(128)S(6)} %pow.3, f32[512,512]{1,0:T(8,128)S(1)} %get-tuple-element.4, f32[]{:T(128)S(6)} %sqrt.3), kind=kOutput, calls=%fused_computation.19 | convolution fusion | flops 1612447744 | bytes 2097160 | tf_op jit(solution)/shard_map/dot_general | solution.py:35
  105.8 1.8 %fusion.88 = f32[512,512]{1,0:T(8,128)S(1)} fusion(f32[512,512]{1,0:T(8,128)S(1)} %fusion.25), kind=kOutput, calls=%fused_computation.91 | convolution fusion | flops 1610612736 | bytes 2097152 | tf_op jit(solution)/shard_map/dot_general | solution.py:38
  107.6 0.0 copy-done.1
  107.6 1.9 %fusion.87 = f32[512,512]{1,0:T(8,128)S(1)} fusion(f32[512,512]{1,0:T(8,128)S(1)} %fusion.88, f32[512,512]{1,0:T(8,128)S(1)} %get-tuple-element.4, f32[]{:T(128)S(6)} %sqrt.3), kind=kOutput, calls=%fused_computation.89 | convolution fusion | flops 1610874880 | bytes 3145732 | tf_op jit(solution)/shard_map/dot_general | solution.py:39
  109.5 1.9 %fusion.21 = f32[512,512]{1,0:T(8,128)S(1)} fusion(f32[512,512]{1,0:T(8,128)S(1)} %fusion.87), kind=kOutput, calls=%fused_computation.27 | convolution fusion | flops 1611661312 | bytes 2097152 | tf_op jit(solution)/shard_map/dot_general | solution.py:37
  111.4 1.9 %fusion.23 = f32[512,512]{1,0:T(8,128)S(1)} fusion(f32[512,512]{1,0:T(8,128)S(1)} %fusion.11, f32[512,512]{1,0:T(8,128)S(1)} %fusion.87), kind=kOutput, calls=%fused_computation.28 | convolution fusion | flops 1611661312 | bytes 3145728 | tf_op jit(solution)/shard_map/dot_general | solution.py:35
  113.3 1.8 %fusion.89 = f32[512,512]{1,0:T(8,128)S(1)} fusion(f32[512,512]{1,0:T(8,128)S(1)} %fusion.21), kind=kOutput, calls=%fused_computation.92 | convolution fusion | flops 1610612736 | bytes 2097152 | tf_op jit(solution)/shard_map/dot_general | solution.py:38
  115.2 2.1 %fusion.90 = f32[512,512]{1,0:T(8,128)S(1)} fusion(f32[512,512]{1,0:T(8,128)S(1)} %fusion.89, f32[512,512]{1,0:T(8,128)S(1)} %fusion.87), kind=kOutput, calls=%fused_computation.93 | convolution fusion | flops 1610612736 | bytes 3145728 | tf_op jit(solution)/shard_map/dot_general | solution.py:39
  117.3 1.9 %fusion.17 = f32[512,512]{1,0:T(8,128)S(1)} fusion(f32[512,512]{1,0:T(8,128)S(1)} %fusion.90), kind=kOutput, calls=%fused_computation.25 | convolution fusion | flops 1611661312 | bytes 2097152 | tf_op jit(solution)/shard_map/dot_general | solution.py:37
  119.2 1.9 %fusion.19 = f32[512,512]{1,0:T(8,128)S(1)} fusion(f32[512,512]{1,0:T(8,128)S(1)} %fusion.23, f32[512,512]{1,0:T(8,128)S(1)} %fusion.90), kind=kOutput, calls=%fused_computation.26 | convolution fusion | flops 1611661312 | bytes 3145728 | tf_op jit(solution)/shard_map/dot_general | solution.py:35
  121.1 1.8 %fusion.91 = f32[512,512]{1,0:T(8,128)S(1)} fusion(f32[512,512]{1,0:T(8,128)S(1)} %fusion.17), kind=kOutput, calls=%fused_computation.94 | convolution fusion | flops 1610612736 | bytes 2097152 | tf_op jit(solution)/shard_map/dot_general | solution.py:38
  123.0 1.8 %fusion.92 = f32[512,512]{1,0:T(8,128)S(1)} fusion(f32[512,512]{1,0:T(8,128)S(1)} %fusion.91, f32[512,512]{1,0:T(8,128)S(1)} %fusion.90), kind=kOutput, calls=%fused_computation.95 | convolution fusion | flops 1610612736 | bytes 3145728 | tf_op jit(solution)/shard_map/dot_general | solution.py:39
  124.8 1.9 %fusion.13 = f32[512,512]{1,0:T(8,128)S(1)} fusion(f32[512,512]{1,0:T(8,128)S(1)} %fusion.92), kind=kOutput, calls=%fused_computation.23 | convolution fusion | flops 1611661312 | bytes 2097152 | tf_op jit(solution)/shard_map/dot_general | solution.py:37
  126.7 1.9 %fusion.15 = f32[512,512]{1,0:T(8,128)S(1)} fusion(f32[512,512]{1,0:T(8,128)S(1)} %fusion.19, f32[512,512]{1,0:T(8,128)S(1)} %fusion.92), kind=kOutput, calls=%fused_computation.24 | convolution fusion | flops 1611661312 | bytes 3145728 | tf_op jit(solution)/shard_map/dot_general | solution.py:35
  128.7 2.1 %fusion.93 = f32[512,512]{1,0:T(8,128)S(1)} fusion(f32[512,512]{1,0:T(8,128)S(1)} %fusion.13), kind=kOutput, calls=%fused_computation.96 | convolution fusion | flops 1610612736 | bytes 2097152 | tf_op jit(solution)/shard_map/dot_general | solution.py:38
  130.8 0.0 copy-start.2
  130.8 1.8 %fusion.1 = f32[512,512]{1,0:T(8,128)S(1)} fusion(f32[512,512]{1,0:T(8,128)S(1)} %fusion.93, f32[512,512]{1,0:T(8,128)S(1)} %fusion.92), kind=kOutput, calls=%fused_computation.7 | convolution fusion | flops 1611661312 | bytes 3145728 | tf_op jit(solution)/shard_map/dot_general | solution.py:39
  132.6 0.0 copy-done.2
  132.7 2.7 %fusion.3 = bf16[1,512,512]{2,1,0:T(8,128)(2,1)} fusion(f32[512,512]{1,0:T(8,128)S(1)} %fusion.15, f32[512,512]{1,0:T(8,128)S(1)} %fusion.1, pred[]{:T(512)} %bitcast.6, bf16[1,512,512]{2,1,0:T(8,128)(2,1)S(1)} %copy-done.2), kind=kOutput, calls=%fused_computation.11 | convolution fusion | flops 1611137024 | bytes 3145729 | tf_op jit(solution)/shard_map/dot_general | solution.py:35
  135.3 0.0 all-to-all-done.2
  135.3 0.3 reshape.34
  135.6 0.7 copy.20
  (1 shorter events, 0.0 us)
Async XLA Ops:
  48.2 25.3 %copy-start.3 = (s32[16]{0:T(128)S(1)}, s32[16]{0:T(128)}, u32[]{:S(2)}) copy-start(s32[16]{0:T(128)} %param.7) | copy-start | bytes 196
  48.2 42.0 %copy-start = (f32[1,512,512]{2,1,0:T(8,128)S(1)}, f32[1,512,512]{2,1,0:T(8,128)}, u32[]{:S(2)}) copy-start(f32[1,512,512]{2,1,0:T(8,128)} %param.5) | copy-start | bytes 3145732
  49.4 40.5 %all-to-all-start.1 = ((bf16[32,16,512]{2,1,0:T(8,128)(2,1)}), bf16[32,16,512]{2,1,0:T(8,128)(2,1)S(1)}, u32[]{:S(2)}, u32[]{:S(2)}) async-start(bf16[32,16,512]{2,1,0:T(8,128)(2,1)} %bitcast.2), calls=%async_computation.1 | async-start | bytes 1048576 | tf_op jit(solution)/shard_map/all_to_all | solution.py:51
  73.1 19.0 %collective-permute-start = (bf16[1,512,512]{2,1,0:T(8,128)(2,1)}, bf16[1,512,512]{2,1,0:T(8,128)(2,1)}, u32[]{:S(2)}, u32[]{:S(2)}) collective-permute-start(bf16[1,512,512]{2,1,0:T(8,128)(2,1)} %param.6), channel_id=1, source_target_pairs={{0,1},{1,0},{2,3},{3,2},{4,5},{5,4},{6,7},{7,6},{8,9},{9,8},{10,11... | collective-permute-start | bytes 1572872 | tf_op jit(solution)/shard_map/ppermute | solution.py:24
  91.4 16.2 %copy-start.1 = (f32[512,512]{1,0:T(8,128)}, f32[512,512]{1,0:T(8,128)S(1)}, u32[]{:S(2)}) copy-start(f32[512,512]{1,0:T(8,128)S(1)} %get-tuple-element.4) | copy-start | bytes 3145732
  98.0 37.4 %all-to-all-start.2 = ((bf16[32,2,2048]{2,1,0:T(2,128)(2,1)}), bf16[32,2,2048]{2,1,0:T(2,128)(2,1)S(1)}, u32[]{:S(2)}, u32[]{:S(2)}) async-start(bf16[32,2,2048]{2,1,0:T(2,128)(2,1)} %reshape.33), calls=%async_computation.2 | async-start | bytes 524288 | tf_op jit(solution)/shard_map/all_to_all | solution.py:61
  130.8 1.9 %copy-start.2 = (bf16[1,512,512]{2,1,0:T(8,128)(2,1)S(1)}, bf16[1,512,512]{2,1,0:T(8,128)(2,1)}, u32[]{:S(2)}) copy-start(bf16[1,512,512]{2,1,0:T(8,128)(2,1)} %param.6) | copy-start | bytes 1572868
where the time goes:
time: 137 us; the launch traced here: 136 us
  blocking collectives  47.6 us (35%)
  matrix products  36.4 us (27%)
  starting transfers between devices  27.9 us (20%)
  waiting for transfers between devices  15.3 us (11%)
  local copies, waits for them, and re-layouts  4.38 us (3%)
  other arithmetic  2.57 us (2%)
  between operations  2.26 us (2%)
    all_to_all x1, blocking collectives, summed_on_arrival(): lax.all_to_all(pieces, axis, split_axis=0, concat_axis=0, tiled=True)  47.6 us
    all_to_all x1, starting transfers between devices, local(): lax.all_to_all(doubled, 'owner', split_axis=0, concat_axis=1, tiled=True)[0]  23.7 us
    all_to_all x1, waiting for transfers between devices, local(): lax.all_to_all(doubled, 'owner', split_axis=0, concat_axis=1, tiled=True)[0]  15.2 us
    dot_general x5, matrix products, inverse_root(): result = jnp.dot(result, factor, precision=lax.Precision.HIGHEST)  10.3 us
    dot_general x4, matrix products, inverse_root(): square = jnp.dot(factor, factor, precision=lax.Precision.HIGHEST)  7.72 us
    dot_general x4, matrix products, inverse_root(): current = jnp.dot(fourth, current, precision=lax.Precision.HIGHEST)  7.65 us
    dot_general x4, matrix products, inverse_root(): fourth = jnp.dot(square, square, precision=lax.Precision.HIGHEST)  7.63 us
    all_to_all x1, starting transfers between devices, local(): lax.all_to_all(portion[None], 'owner', split_axis=1, concat_axis=0, tiled...  3.85 us
  transfers between devices with their start and end apart: 3, of which 1 were waited for; matrix products, arithmetic and copies ran while one was open for 26% of the time, Pallas kernels for 0%

commit v1 on v0

--- a/solution.py
+++ b/solution.py
@@ -5,6 +5,13 @@
 
 ITERS = 5
 BETA = 0.8
+
+
+def stacked_exchange(x, name, split, join):
+    size = lax.axis_size(name)
+    blocks = jnp.stack(jnp.split(x, size, axis=split), axis=0)
+    blocks = lax.all_to_all(blocks, name, split_axis=0, concat_axis=0)
+    return jnp.concatenate(blocks, axis=join)
 
 
 def split_up(x, dim, peers):
@@ -48,7 +55,7 @@
     side = owner % 2
     flag = lax.dynamic_index_in_dim(refresh, owner // 2, 0, keepdims=False)
     doubled = jnp.repeat(grad, 2, axis=0)
-    whole = lax.all_to_all(doubled, "owner", split_axis=0, concat_axis=1, tiled=True)[0]
+    whole = stacked_exchange(doubled, "owner", 0, 1)[0]
     oriented = jnp.where(side == 0, whole, whole.T)
     gram = jnp.dot(oriented, oriented.T, preferred_element_type=jnp.float32)
     partner = partner_2(roots, "owner", 0)[0]

time: 137 us -> 156 us (1.14)
  local copies, waits for them, and re-layouts: 4.38 us -> 23 us
    unnamed x12 -> x41, local copies, waits for them, and re-layouts: 1.61 us -> 20.4 us
  transfers between devices with their start and end apart: 3 -> 3, of which waited for: 1 -> 1; matrix products, arithmetic and copies ran while one was open for 26% -> 23% of each run, Pallas kernels for 0% -> 0%
where the time goes in v1:
time: 156 us
  blocking collectives  47.6 us (31%)
  matrix products  37.5 us (24%)
  starting transfers between devices  27.9 us (18%)
  local copies, waits for them, and re-layouts  23 us (15%)
  waiting for transfers between devices  15.3 us (10%)
  other arithmetic  2.57 us (2%)
  between operations  2.28 us (1%)
    all_to_all x1, blocking collectives, summed_on_arrival(): lax.all_to_all(pieces, axis, split_axis=0, concat_axis=0, tiled=True)  47.6 us
    all_to_all x1, starting transfers between devices, stacked_exchange(): blocks = lax.all_to_all(blocks, name, split_axis=0, concat_axis=0)  23.7 us
    unnamed x41, local copies, waits for them, and re-layouts  20.4 us
    all_to_all x1, waiting for transfers between devices, stacked_exchange(): blocks = lax.all_to_all(blocks, name, split_axis=0, concat_axis=0)  15.2 us
    dot_general x5, matrix products, inverse_root(): result = jnp.dot(result, factor, precision=lax.Precision.HIGHEST)  11.3 us
    dot_general x4, matrix products, inverse_root(): square = jnp.dot(factor, factor, precision=lax.Precision.HIGHEST)  7.72 us
    dot_general x4, matrix products, inverse_root(): current = jnp.dot(fourth, current, precision=lax.Precision.HIGHEST)  7.65 us
    dot_general x4, matrix products, inverse_root(): fourth = jnp.dot(square, square, precision=lax.Precision.HIGHEST)  7.63 us
  transfers between devices with their start and end apart: 3, of which 1 were waited for; matrix products, arithmetic and copies ran while one was open for 23% of the time, Pallas kernels for 0%

profile of v1, /device:TPU:1, one launch (start us, length us, event | category | flops | bytes accessed | tf_op | source)
XLA Modules:
  0.0 156.0 jit_solution(7133277278637817041)
XLA Ops:
  0.6 47.6 %all_to_all.19 = bf16[8,1,16,16,512]{4,3,2,1,0:T(8,128)(2,1)S(1)} all-to-all(bf16[8,1,16,16,512]{4,3,2,1,0:T(8,128)(2,1)} %bitcast.217), channel_id=1, replica_groups=mesh['dp'=8,'owner'=32] {'dp'}, dimensions={0} | all-to-all | bytes 4194304 | tf_op jit(solution)/shard_map/all_to_all | solution.py:24
  48.2 0.4 reduce_sum.21
  48.6 0.6 constant_dynamic-update-slice_fusion.31
  49.3 0.6 constant_dynamic-update-slice_fusion.30
  49.9 0.6 constant_dynamic-update-slice_fusion.29
  50.5 0.6 constant_dynamic-update-slice_fusion.28
  51.1 0.6 constant_dynamic-update-slice_fusion.27
  51.7 0.6 constant_dynamic-update-slice_fusion.26
  52.3 0.6 constant_dynamic-update-slice_fusion.25
  52.9 0.6 constant_dynamic-update-slice_fusion.24
  53.5 0.6 constant_dynamic-update-slice_fusion.23
  54.1 0.6 constant_dynamic-update-slice_fusion.22
  54.7 0.6 constant_dynamic-update-slice_fusion.21
  55.3 0.6 constant_dynamic-update-slice_fusion.20
  55.9 0.6 constant_dynamic-update-slice_fusion.19
  56.5 0.6 constant_dynamic-update-slice_fusion.18
  57.1 0.6 constant_dynamic-update-slice_fusion.17
  57.7 0.6 constant_dynamic-update-slice_fusion.16
  58.4 0.6 constant_dynamic-update-slice_fusion.15
  59.0 0.6 constant_dynamic-update-slice_fusion.14
  59.6 0.6 constant_dynamic-update-slice_fusion.13
  60.2 0.6 constant_dynamic-update-slice_fusion.12
  60.8 0.6 constant_dynamic-update-slice_fusion.11
  61.4 0.6 constant_dynamic-update-slice_fusion.10
  62.0 0.6 constant_dynamic-update-slice_fusion.9
  62.6 0.6 constant_dynamic-update-slice_fusion.8
  63.2 0.6 constant_dynamic-update-slice_fusion.7
  63.8 0.6 constant_dynamic-update-slice_fusion.6
  64.4 0.6 constant_dynamic-update-slice_fusion.5
  65.0 0.6 constant_dynamic-update-slice_fusion.4
  65.6 0.6 constant_dynamic-update-slice_fusion.3
  66.2 0.6 constant_dynamic-update-slice_fusion.2
  66.9 0.6 constant_dynamic-update-slice_fusion.1
  67.5 0.6 constant_dynamic-update-slice_fusion
  68.1 23.7 %all-to-all-start.1 = ((bf16[32,1,16,512]{3,2,1,0:T(8,128)(2,1)}), bf16[32,1,16,512]{3,2,1,0:T(8,128)(2,1)S(1)}, u32[]{:S(2)}, u32[]{:S(2)}) async-start(bf16[32,1,16,512]{3,2,1,0:T(8,128)(2,1)} %constant_dynamic-update-slice_fusion), calls=%async_computation.1 | async-start | bytes 1048576 | tf_op jit(solution)/shard_map/all_to_all | solution.py:13
  91.8 0.3 collective-permute-start
  92.1 0.6 dynamic_slice.7
  93.3 15.2 %all-to-all-done.1 = bf16[32,1,16,512]{3,2,1,0:T(8,128)(2,1)S(1)} async-done(((bf16[32,1,16,512]{3,2,1,0:T(8,128)(2,1)}), bf16[32,1,16,512]{3,2,1,0:T(8,128)(2,1)S(1)}, u32[]{:S(2)}, u32[]{:S(2)}) %all-to-all-start.1) | async-done | bytes 524320 | tf_op jit(solution)/shard_map/all_to_all | solution.py:13
  108.8 1.2 multiply_reduce_fusion
  110.8 1.9 %fusion.6 = bf16[1,512,256]{2,1,0:T(8,128)(2,1)S(1)} fusion(bf16[512,512]{1,0:T(8,128)(2,1)S(1)} %bitcast.183, bf16[1,512,512]{2,1,0:T(8,128)(2,1)} %param.6, bf16[1,512,512]{2,1,0:T(8,128)(2,1)} %collective-permute-done, pred[]{:T(512)S(6)} %eq.26, bf16[512,512]{1,0:T(8,128)(2,1)} %bitcast.39, s32[]{:T(128)S(6)} %select_n.56, bf16[512,512]{1,0:T(8,128)(2,1)} %bitcast.42), kind=kOutput, calls=%fused_computation.14 | convolution fusion | flops 403439616 | bytes 2360832 | tf_op jit(solution)/shard_map/dot_general | solution.py:67
  112.7 0.4 copy.53
  113.1 0.5 broadcast.126
  113.6 2.2 %reduce.2 = bf16[512,256]{1,0:T(8,128)(2,1)S(1)} reduce(bf16[512,1,256]{2,1,0:T(2,128)(2,1)S(1)} %bitcast.218, bf16[]{:T(256)} %broadcast.126), dimensions={1}, to_apply=%bitcast.180.reduce_sub_computation | reduce | bytes 524290
  115.8 0.8 reshape.29
  116.6 3.9 %all-to-all-start.2 = ((bf16[32,2,2048]{2,1,0:T(2,128)(2,1)}), bf16[32,2,2048]{2,1,0:T(2,128)(2,1)S(1)}, u32[]{:S(2)}, u32[]{:S(2)}) async-start(bf16[32,2,2048]{2,1,0:T(2,128)(2,1)} %reshape.29), calls=%async_computation.2 | async-start | bytes 524288 | tf_op jit(solution)/shard_map/all_to_all | solution.py:68
  120.5 2.0 %fusion.25 = f32[512,512]{1,0:T(8,128)S(1)} fusion(f32[512,512]{1,0:T(8,128)S(1)} %get-tuple-element.4, f32[]{:T(128)S(6)} %sqrt.3), kind=kOutput, calls=%fused_computation.29 | convolution fusion | flops 1611923456 | bytes 2097156 | tf_op jit(solution)/shard_map/dot_general | solution.py:44
  122.5 1.9 %fusion.11 = f32[512,512]{1,0:T(8,128)S(1)} fusion(f32[]{:T(128)S(6)} %pow.3, f32[512,512]{1,0:T(8,128)S(1)} %get-tuple-element.4, f32[]{:T(128)S(6)} %sqrt.3), kind=kOutput, calls=%fused_computation.19 | convolution fusion | flops 1612447744 | bytes 2097160 | tf_op jit(solution)/shard_map/dot_general | solution.py:42
  124.4 1.8 %fusion.88 = f32[512,512]{1,0:T(8,128)S(1)} fusion(f32[512,512]{1,0:T(8,128)S(1)} %fusion.25), kind=kOutput, calls=%fused_computation.155 | convolution fusion | flops 1610612736 | bytes 2097152 | tf_op jit(solution)/shard_map/dot_general | solution.py:45
  126.3 1.9 %fusion.87 = f32[512,512]{1,0:T(8,128)S(1)} fusion(f32[512,512]{1,0:T(8,128)S(1)} %fusion.88, f32[512,512]{1,0:T(8,128)S(1)} %get-tuple-element.4, f32[]{:T(128)S(6)} %sqrt.3), kind=kOutput, calls=%fused_computation.153 | convolution fusion | flops 1610874880 | bytes 3145732 | tf_op jit(solution)/shard_map/dot_general | solution.py:46
  128.1 1.9 %fusion.21 = f32[512,512]{1,0:T(8,128)S(1)} fusion(f32[512,512]{1,0:T(8,128)S(1)} %fusion.87), kind=kOutput, calls=%fused_computation.27 | convolution fusion | flops 1611661312 | bytes 2097152 | tf_op jit(solution)/shard_map/dot_general | solution.py:44
  130.1 1.9 %fusion.23 = f32[512,512]{1,0:T(8,128)S(1)} fusion(f32[512,512]{1,0:T(8,128)S(1)} %fusion.11, f32[512,512]{1,0:T(8,128)S(1)} %fusion.87), kind=kOutput, calls=%fused_computation.28 | convolution fusion | flops 1611661312 | bytes 3145728 | tf_op jit(solution)/shard_map/dot_general | solution.py:42
  132.0 1.8 %fusion.89 = f32[512,512]{1,0:T(8,128)S(1)} fusion(f32[512,512]{1,0:T(8,128)S(1)} %fusion.21), kind=kOutput, calls=%fused_computation.156 | convolution fusion | flops 1610612736 | bytes 2097152 | tf_op jit(solution)/shard_map/dot_general | solution.py:45
  133.8 2.1 %fusion.90 = f32[512,512]{1,0:T(8,128)S(1)} fusion(f32[512,512]{1,0:T(8,128)S(1)} %fusion.89, f32[512,512]{1,0:T(8,128)S(1)} %fusion.87), kind=kOutput, calls=%fused_computation.157 | convolution fusion | flops 1610612736 | bytes 3145728 | tf_op jit(solution)/shard_map/dot_general | solution.py:46
  135.9 1.9 %fusion.17 = f32[512,512]{1,0:T(8,128)S(1)} fusion(f32[512,512]{1,0:T(8,128)S(1)} %fusion.90), kind=kOutput, calls=%fused_computation.25 | convolution fusion | flops 1611661312 | bytes 2097152 | tf_op jit(solution)/shard_map/dot_general | solution.py:44
  137.8 1.9 %fusion.19 = f32[512,512]{1,0:T(8,128)S(1)} fusion(f32[512,512]{1,0:T(8,128)S(1)} %fusion.23, f32[512,512]{1,0:T(8,128)S(1)} %fusion.90), kind=kOutput, calls=%fused_computation.26 | convolution fusion | flops 1611661312 | bytes 3145728 | tf_op jit(solution)/shard_map/dot_general | solution.py:42
  139.7 1.8 %fusion.91 = f32[512,512]{1,0:T(8,128)S(1)} fusion(f32[512,512]{1,0:T(8,128)S(1)} %fusion.17), kind=kOutput, calls=%fused_computation.158 | convolution fusion | flops 1610612736 | bytes 2097152 | tf_op jit(solution)/shard_map/dot_general | solution.py:45
  141.6 1.8 %fusion.92 = f32[512,512]{1,0:T(8,128)S(1)} fusion(f32[512,512]{1,0:T(8,128)S(1)} %fusion.91, f32[512,512]{1,0:T(8,128)S(1)} %fusion.90), kind=kOutput, calls=%fused_computation.159 | convolution fusion | flops 1610612736 | bytes 3145728 | tf_op jit(solution)/shard_map/dot_general | solution.py:46
  143.5 1.9 %fusion.13 = f32[512,512]{1,0:T(8,128)S(1)} fusion(f32[512,512]{1,0:T(8,128)S(1)} %fusion.92), kind=kOutput, calls=%fused_computation.23 | convolution fusion | flops 1611661312 | bytes 2097152 | tf_op jit(solution)/shard_map/dot_general | solution.py:44
  145.4 1.9 %fusion.15 = f32[512,512]{1,0:T(8,128)S(1)} fusion(f32[512,512]{1,0:T(8,128)S(1)} %fusion.19, f32[512,512]{1,0:T(8,128)S(1)} %fusion.92), kind=kOutput, calls=%fused_computation.24 | convolution fusion | flops 1611661312 | bytes 3145728 | tf_op jit(solution)/shard_map/dot_general | solution.py:42
  147.3 2.1 %fusion.93 = f32[512,512]{1,0:T(8,128)S(1)} fusion(f32[512,512]{1,0:T(8,128)S(1)} %fusion.13), kind=kOutput, calls=%fused_computation.160 | convolution fusion | flops 1610612736 | bytes 2097152 | tf_op jit(solution)/shard_map/dot_general | solution.py:45
  149.4 1.9 %fusion.1 = f32[512,512]{1,0:T(8,128)S(1)} fusion(f32[512,512]{1,0:T(8,128)S(1)} %fusion.93, f32[512,512]{1,0:T(8,128)S(1)} %fusion.92), kind=kOutput, calls=%fused_computation.7 | convolution fusion | flops 1611661312 | bytes 3145728 | tf_op jit(solution)/shard_map/dot_general | solution.py:46
  151.3 3.7 %fusion.3 = bf16[1,512,512]{2,1,0:T(8,128)(2,1)} fusion(f32[512,512]{1,0:T(8,128)S(1)} %fusion.15, f32[512,512]{1,0:T(8,128)S(1)} %fusion.1, pred[]{:T(512)} %bitcast.38, bf16[1,512,512]{2,1,0:T(8,128)(2,1)} %param.6), kind=kOutput, calls=%fused_computation.11 | convolution fusion | flops 1611137024 | bytes 3145729 | tf_op jit(solution)/shard_map/dot_general | solution.py:42
  155.0 0.3 reshape.30
  155.3 0.7 copy.51
  (11 shorter events, 0.3 us)
Async XLA Ops:
  48.2 43.9 %copy-start.2 = (s32[16]{0:T(128)S(1)}, s32[16]{0:T(128)}, u32[]{:S(2)}) copy-start(s32[16]{0:T(128)} %param.7) | copy-start | bytes 196
  48.6 60.2 %copy-start = (f32[1,512,512]{2,1,0:T(8,128)S(1)}, f32[1,512,512]{2,1,0:T(8,128)}, u32[]{:S(2)}) copy-start(f32[1,512,512]{2,1,0:T(8,128)} %param.5) | copy-start | bytes 3145732
  68.1 40.5 %all-to-all-start.1 = ((bf16[32,1,16,512]{3,2,1,0:T(8,128)(2,1)}), bf16[32,1,16,512]{3,2,1,0:T(8,128)(2,1)S(1)}, u32[]{:S(2)}, u32[]{:S(2)}) async-start(bf16[32,1,16,512]{3,2,1,0:T(8,128)(2,1)} %constant_dynamic-update-slice_fusion), calls=%async_computation.1 | async-start | bytes 1048576 | tf_op jit(solution)/shard_map/all_to_all | solution.py:13
  91.8 19.0 %collective-permute-start = (bf16[1,512,512]{2,1,0:T(8,128)(2,1)}, bf16[1,512,512]{2,1,0:T(8,128)(2,1)}, u32[]{:S(2)}, u32[]{:S(2)}) collective-permute-start(bf16[1,512,512]{2,1,0:T(8,128)(2,1)} %param.6), channel_id=1, source_target_pairs={{0,1},{1,0},{2,3},{3,2},{4,5},{5,4},{6,7},{7,6},{8,9},{9,8},{10,11... | collective-permute-start | bytes 1572872 | tf_op jit(solution)/shard_map/ppermute | solution.py:31
  110.1 16.2 %copy-start.1 = (f32[512,512]{1,0:T(8,128)}, f32[512,512]{1,0:T(8,128)S(1)}, u32[]{:S(2)}) copy-start(f32[512,512]{1,0:T(8,128)S(1)} %get-tuple-element.4) | copy-start | bytes 3145732
  116.6 38.4 %all-to-all-start.2 = ((bf16[32,2,2048]{2,1,0:T(2,128)(2,1)}), bf16[32,2,2048]{2,1,0:T(2,128)(2,1)S(1)}, u32[]{:S(2)}, u32[]{:S(2)}) async-start(bf16[32,2,2048]{2,1,0:T(2,128)(2,1)} %reshape.29), calls=%async_computation.2 | async-start | bytes 524288 | tf_op jit(solution)/shard_map/all_to_all | solution.py:68
